TPU v7x, 512 devices: a whole 4x4x16 slice. The times are simulated.
512 devices in a mesh: rep: 8 (over x, z_hi), zero: 64 (over z_lo, y, core).
Axes of the slice: x: 4, y: 4, z: 16 (z_hi: 2, z_lo: 8; z = z_hi * 8 + z_lo), core: 2. Of those that a mesh axis runs over, the one named last changes fastest.
Arguments:
- pooled: bfloat16 [65536, 768], P(('rep', 'zero')), may hold values from -24 to 24
- text_embed: bfloat16 [65536, 768], P(('rep', 'zero')), may hold values from -6 to 6
- head_weight: bfloat16 [768, 768], P('zero'), may hold values from -0.21875 to 0.21875
- natural_exponent_factor: float32 [1], replicated, may hold values from 3.4 to 4
- logit_bias: float32 [1], replicated, may hold values from -10 to -8
Outputs:
- row_loss: float32 [65536], P(('rep', 'zero'))
- feat_grad: bfloat16 [65536, 768], P(('rep', 'zero'))
- weight_grad: float32 [768, 768], P('zero')
- scale_grads: float32 [2], replicated
All inputs are finite; a program needn't handle non-finite values.
Results may differ from a plain program's by a relative error of at most 0.015.
Values may be sent and summed in bfloat16 or wider, within the bound.
A program may use at most 64 MiB of HBM per device.

v0:
```python
import jax
import jax.numpy as jnp
from jax import lax
from jax.sharding import PartitionSpec as P


def patch_penalty_entries(
    picture_sample_slab,
    caption_sample_slab,
    matching_pair_sign,
    inverse_warmth_factor,
    offset_count,
):
    cosine_matrix_entries = lax.dot_general(
        picture_sample_slab,
        caption_sample_slab,
        (((1,), (1,)), ((), ())),
        preferred_element_type=jnp.float32,
    )
    multiplied_affinities = inverse_warmth_factor * cosine_matrix_entries
    logits = multiplied_affinities + offset_count
    polarity = jnp.where(matching_pair_sign, 1.0, -1.0).astype(jnp.float32)
    row_losses = jnp.sum(jax.nn.softplus(-polarity * logits), axis=1)
    squashing_derivatives = -polarity * jax.nn.sigmoid(-polarity * logits)
    temp_total = jnp.sum(squashing_derivatives * multiplied_affinities)
    bias_total = jnp.sum(squashing_derivatives)
    upstream_derivative = inverse_warmth_factor * jnp.dot(
        squashing_derivatives.astype(jnp.bfloat16),
        caption_sample_slab,
        preferred_element_type=jnp.float32,
    )
    return (row_losses, upstream_derivative, temp_total, bias_total)


def per_device(pooled, text_embed, head_weight, natural_exponent_factor, logit_bias):
    batch_rows = pooled.shape[0]
    inverse_warmth_factor = jnp.exp(natural_exponent_factor[0])
    offset_count = logit_bias[0]
    full_weight = lax.all_gather(head_weight, "zero", axis=0, tiled=True)
    projected = jnp.dot(pooled, full_weight, preferred_element_type=jnp.float32)
    inverse = lax.rsqrt(jnp.sum(projected * projected, axis=1, keepdims=True) + 1e-06)
    img_unit = projected * inverse
    picture_bfloat_copy = img_unit.astype(jnp.bfloat16)
    text_float = text_embed.astype(jnp.float32)
    txt_bf = (
        text_float * lax.rsqrt(jnp.sum(text_float * text_float, axis=1, keepdims=True) + 1e-06)
    ).astype(jnp.bfloat16)
    position = lax.axis_index("zero")
    mine = position * batch_rows + jnp.arange(batch_rows, dtype=jnp.int32)
    portion_ratio = lax.all_gather(txt_bf, "zero", axis=0, tiled=True)
    columns = jnp.arange(portion_ratio.shape[0], dtype=jnp.int32)
    matching_pair_sign = mine[:, None] == columns[None, :]
    losses, upstream_derivative, temp_part, bias_part = patch_penalty_entries(
        picture_bfloat_copy, portion_ratio, matching_pair_sign, inverse_warmth_factor, offset_count
    )
    scale_grads = lax.psum(jnp.stack([temp_part, bias_part]), ("rep", "zero"))
    grad_proj = (
        (
            upstream_derivative
            - img_unit * jnp.sum(img_unit * upstream_derivative, axis=1, keepdims=True)
        )
        * inverse
    ).astype(jnp.bfloat16)
    feat_grad = lax.dot_general(
        grad_proj, full_weight, (((1,), (1,)), ((), ())), preferred_element_type=jnp.float32
    ).astype(jnp.bfloat16)
    columns = pooled
    shard_rows = lax.psum_scatter(
        lax.dot_general(
            columns, grad_proj, (((0,), (0,)), ((), ())), preferred_element_type=jnp.float32
        ),
        "zero",
        scatter_dimension=0,
        tiled=True,
    )
    weight_grad = lax.psum(shard_rows.astype(jnp.bfloat16), "rep").astype(jnp.float32)
    return (losses, feat_grad, weight_grad, scale_grads)


def solution(mesh):
    return jax.shard_map(
        per_device,
        mesh=mesh,
        in_specs=(P(("rep", "zero"), None), P(("rep", "zero"), None), P("zero", None), P(), P()),
        out_specs=(P(("rep", "zero")), P(("rep", "zero"), None), P("zero", None), P()),
        check_vma=False,
    )
```

profile of v0, /device:TPU:1, one launch (start us, length us, event | category | flops | bytes accessed | tf_op | source)
XLA Modules:
  0.0 918.0 jit_solution(4494285878160524980)
XLA Ops:
  7.2 0.0 copy-start
  7.2 0.0 all-gather.6.cloned.1.call-start
  7.2 0.7 all-gather.6.cloned.1.call-update
  7.9 0.0 all-gather.4.cloned.1.call-start
  8.0 1.0 fusion.6
  9.0 1.7 fusion.7
  10.7 0.0 all-gather.4.cloned.1.call-update
  12.1 1.3 dynamic-slice
  14.0 122.2 %all-gather.6.cloned.1.call-done = bf16[64,12,768]{2,1,0:T(8,128)(2,1)} async-done(((bf16[1,12,768]{2,1,0:T(8,128)(2,1)}), bf16[64,12,768]{2,1,0:T(8,128)(2,1)}) %all-gather.6.cloned.1.call-update) | async-done | bytes 1179664 | tf_op jit(solution)/shard_map/all_gather | solution.py:39
  136.3 2.2 reshape.27
  138.5 0.0 copy-done
  138.5 0.4 multiply_reduce_fusion.2
  139.0 130.1 %all-gather.4.cloned.1.call-done = bf16[8192,768]{1,0:T(8,128)(2,1)} async-done(((bf16[128,768]{1,0:T(8,128)(2,1)}), bf16[8192,768]{1,0:T(8,128)(2,1)}) %all-gather.4.cloned.1.call-update) | async-done | bytes 12582928 | tf_op jit(solution)/shard_map/all_gather | solution.py:50
  269.1 0.0 copy-start.1
  269.1 11.6 %multiply_reduce_fusion = (f32[]{:T(128)}, f32[]{:T(128)}, f32[128]{0:T(128)}, f32[128,8192]{1,0:T(8,128)S(1)}) fusion(f32[]{:T(128)} %bitcast.19, s32[128]{0:T(128)S(1)} %iota_add_fusion, bf16[8192,768]{1,0:T(8,128)(2,1)} %all-gather.4.cloned.1.call-done, f32[128,768]{1,0:T(8,128)S(1)} %get-tuple-element.20, f32[128]{0:T(128)S(1)} %add_rsqrt_fusion.1, f32[]{:T(128)} %bitcast), kind=kOutput, calls=%fused_computation.3 | convolution fusion | flops 1631780736 | bytes 17171984 | tf_op jit(solution)/shard_map/dot_general | solution.py:14
  280.7 0.0 copy-done.1
  280.7 3.0 multiply_reduce_fusion.1
  283.7 0.2 multiply_convert_fusion
  283.9 1.9 convolution_bitcast_fusion
  285.8 1.2 convolution_convert_fusion
  287.0 439.5 %all-reduce.2 = bf16[768,768]{0,1:T(8,128)(2,1)S(1)} all-reduce(f32[768,768]{0,1:T(8,128)} %convolution_bitcast_fusion), channel_id=2, replica_groups=mesh['rep'=8,'zero'=64] {'zero'}, use_global_device_ids=true, to_apply=%region_4.5.clone | all-reduce | flops 589824 | bytes 3538944
  726.5 0.1 dynamic-slice_convert_fusion
  726.6 70.6 %psum.14 = bf16[12,768]{0,1:T(8,128)(2,1)S(1)} all-reduce(bf16[12,768]{0,1:T(8,128)(2,1)S(1)} %dynamic-slice_convert_fusion), channel_id=1, replica_groups=mesh['rep'=8,'zero'=64] {'rep'}, use_global_device_ids=true, to_apply=%region_5.6 | all-reduce | flops 9216 | bytes 36864 | tf_op jit(solution)/shard_map/psum | solution.py:76
  797.2 1.4 pad_maximum_fusion
  798.6 0.7 copy.11
  799.3 111.8 %psum.15 = f32[2]{0:T(128)} all-reduce(f32[2]{0:T(128)S(1)} %pad_maximum_fusion), channel_id=1, replica_groups=mesh['rep'=8,'zero'=64] {'rep','zero'}, use_global_device_ids=true, to_apply=%region_8.9 | all-reduce | flops 2 | bytes 16 | tf_op jit(solution)/shard_map/psum | solution.py:56
  (3 shorter events, 0.0 us)
Async XLA Ops:
  7.2 131.4 %copy-start = (bf16[128,768]{1,0:T(8,128)(2,1)S(1)}, bf16[128,768]{1,0:T(8,128)(2,1)}, u32[]{:S(2)}) copy-start(bf16[128,768]{1,0:T(8,128)(2,1)} %param.5) | copy-start | bytes 589828
  7.2 129.1 %all-gather.6.cloned.1.call-start = ((), (), s32[]{:S(2)}) async-start(), calls=%async_computation.1 | async-start | bytes 1597440 | tf_op jit(solution)/shard_map/all_gather | solution.py:39
  7.9 261.2 %all-gather.4.cloned.1.call-start = ((), (), s32[]{:S(2)}) async-start(), calls=%async_computation | async-start | bytes 12779520 | tf_op jit(solution)/shard_map/all_gather | solution.py:50
  269.1 11.6 %copy-start.1 = (bf16[8192,768]{1,0:T(8,128)(2,1)S(1)}, bf16[8192,768]{1,0:T(8,128)(2,1)}, u32[]{:S(2)}) copy-start(bf16[8192,768]{1,0:T(8,128)(2,1)} %all-gather.4.cloned.1.call-done) | copy-start | bytes 37748740
Sparse Core Ops, SparseCore 0:
  10.2 126.0 all-gather.5
  139.0 130.0 all-gather.3
where the time goes:
time: 918 us
  blocking collectives  622 us (68%)
  waiting for transfers between devices  253 us (28%)
  matrix products  18.2 us (2%)
  between operations  16.1 us (2%)
    unnamed x1, blocking collectives  439 us
    all_gather x1, waiting for transfers between devices, per_device(): portion_ratio = lax.all_gather(txt_bf, 'zero', axis=0, tiled=True)  130 us
    all_gather x1, waiting for transfers between devices, per_device(): full_weight = lax.all_gather(head_weight, 'zero', axis=0, tiled=True)  122 us
    psum x1, blocking collectives, per_device(): scale_grads = lax.psum(jnp.stack([temp_part, bias_part]), ('rep', 'zero'))  112 us
    psum x1, blocking collectives, per_device(): lax.psum(shard_rows.astype(jnp.bfloat16), 'rep').astype(jnp.float32)  70.6 us
  transfers between devices with their start and end apart: 2, of which 2 were waited for; matrix products, arithmetic and copies ran while one was open for 1% of the time, Pallas kernels for 0%

commit v1 on v0

v1 whole, which is shorter than its diff:
```python
import jax
import jax.numpy as jnp
from jax import lax
from jax.experimental import pallas as pl
from jax.experimental.pallas import tpu as pltpu
from jax.sharding import PartitionSpec as P

MESH = pl.DeviceIdType.MESH
F32 = jnp.float32
BF = jnp.bfloat16


def dev(x, zh, zl, y, c):
    return (x * 2 + zh, zl * 8 + y * 2 + c)


def rem(a, n):
    return lax.rem(a, jnp.int32(n))


def div(a, n):
    return lax.div(a, jnp.int32(n))


def nn(a, b):
    return jnp.dot(a, b, preferred_element_type=F32)


def nt(a, b):
    return lax.dot_general(a, b, (((1,), (1,)), ((), ())), preferred_element_type=F32)


def kernel(
    p_ref, t_ref, w_ref, nat_ref, bias_ref,
    loss_ref, feat_ref, wg_ref, sc_ref,
    txt, pool, wgat, sel, selt, wc, pt, iu, inv, img, s_scr, slope_scr, acc, loss_acc, tot_acc,
    gp, fsend, frecv, lbuf, cs, cbuf, xs, xbuf, ysum, zs, zbuf, agb, abuf, s2buf, s3buf,
    t_rs, t_sr, t_sl, t_ss, p_rs, p_s, wz_rs, wz_s, wx_rs, wx_s, wy_rs, wy_s, wc_rs, wc_s,
    f_rs, f_s, l_rs, l_s, c_rs, c_s, x_rs, x_s, z_rs, z_s, a_rs, a_s, s2_rs, s2_s, s3_rs, s3_s,
):
    rep = lax.axis_index("rep")
    zero = lax.axis_index("zero")
    x, zh = div(rep, 2), rem(rep, 2)
    zl, y, c = div(zero, 8), rem(div(zero, 2), 4), rem(zero, 2)
    oc = 1 - c
    temp = jnp.exp(jnp.full((8, 128), nat_ref[0], F32))[0:1, 0:1]
    bias = bias_ref[0]

    def rc(src, dst, ss, rs, to):
        return pltpu.make_async_remote_copy(src, dst, ss, rs, device_id=to, device_id_type=MESH)

    bar = pltpu.get_barrier_semaphore()

    def sig(to):
        pl.semaphore_signal(bar, inc=1, device_id=to, device_id_type=MESH)

    wgat[y, c, zl] = jnp.zeros((16, 768), BF)
    wgat[y, c, zl, 0:12] = w_ref[...]
    sig(dev(x, zh, zl, y, oc))
    for k in (1, 2, 3):
        sig(dev(x, zh, zl, rem(y + k, 4), c))
        sig(dev(rem(x + k, 4), zh, zl, y, c))
        sig(dev(rem(x + k, 4), 1 - zh, zl, y, c))
    for k in range(1, 8):
        sig(dev(x, zh, rem(zl + k, 8), y, c))
    sig(dev(x, 1 - zh, zl, y, c))

    def ag_self(k):
        return (div(k, 4) == x) & (rem(div(k, 2), 2) == zh) & (x == y) & (rem(k, 2) == c)

    def ag_from_self(k):
        return (x == y) & (div(k, 4) == y) & (rem(div(k, 2), 2) == zh) & (rem(k, 2) == c)

    tf = t_ref[...].astype(F32)
    txt[zl, c] = (tf * lax.rsqrt(jnp.sum(tf * tf, axis=1, keepdims=True) + 1e-06)).astype(BF)
    pl.semaphore_wait(bar, 18)

    def tpiece(slot, cc, h):
        return txt.at[slot, cc, pl.ds(h * 64, 64)]

    def t_right(slot, h):
        return rc(tpiece(slot, c, h), tpiece(slot, c, h), t_sr.at[slot, h], t_rs.at[slot, c, h], dev(x, zh, zl + 1, y, c))

    def t_left(slot, h):
        return rc(tpiece(slot, c, h), tpiece(slot, c, h), t_sl.at[slot, h], t_rs.at[slot, c, h], dev(x, zh, zl - 1, y, c))

    def t_sib(slot, h):
        return rc(tpiece(slot, c, h), tpiece(slot, c, h), t_ss.at[slot, h], t_rs.at[slot, c, h], dev(x, zh, zl, y, oc))

    def t_wait(slot, cc, h):
        rc(tpiece(slot, cc, h), tpiece(slot, cc, h), t_ss.at[slot, h], t_rs.at[slot, cc, h], dev(x, zh, zl, y, oc)).wait_recv()

    def wz(k_to, slot):
        piece = wgat.at[y, c, slot, :, pl.ds(pl.multiple_of(x * 256, 256), 256)]
        return rc(piece, piece, wz_s.at[k_to], wz_rs.at[slot], dev(x, zh, k_to, y, c))

    def wx(xt, slot):
        piece = wgat.at[y, c, :, :, pl.ds(pl.multiple_of(slot * 256, 256), 256)]
        return rc(piece, piece, wx_s.at[xt], wx_rs.at[slot], dev(xt, zh, zl, y, c))

    def pcopy(yt, slot):
        return rc(p_ref, pool.at[slot], p_s.at[yt], p_rs.at[slot], dev(x, zh, zl, yt, c))

    @pl.when(x < 3)
    def _():
        for k in range(1, 8):
            wz(rem(zl + k, 8), zl).start()
    for h in (0, 1):
        @pl.when(zl < 7)
        def _():
            t_right(zl, h).start()

        @pl.when(zl > 0)
        def _():
            t_left(zl, h).start()
    for h in (0, 1):
        t_sib(zl, h).start()

    for k in (1, 3, 2):
        pcopy(rem(y + k, 4), y).start()

    def forward(d):
        pass
        for h in (0, 1):
            @pl.when(zl - d >= 0)
            def _():
                t_wait(zl - d, c, h)

                @pl.when(zl < 7)
                def _():
                    t_right(zl - d, h).start()
                t_sib(zl - d, h).start()

            @pl.when(zl + d <= 7)
            def _():
                t_wait(zl + d, c, h)

                @pl.when(zl > 0)
                def _():
                    t_left(zl + d, h).start()
                t_sib(zl + d, h).start()

    pool[y] = p_ref[...]

    def where_row(k):
        r = k % 16
        return jnp.where(r < 12, 96 * ((k // 16) % 8) + 12 * (k // 128) + r, -1)

    cols = where_row(lax.broadcasted_iota(jnp.int32, (1, 1024), 1))

    def body(i, _):
        rows = lax.broadcasted_iota(jnp.int32, (128, 1), 0) + i * 128
        sel[pl.ds(i * 128, 128), :] = jnp.where(rows == cols, 1.0, 0.0).astype(BF)
        return 0
    lax.fori_loop(0, 6, body, 0)
    lanes = lax.broadcasted_iota(jnp.int32, (1, 768), 1)

    def body(i, _):
        rows = where_row(lax.broadcasted_iota(jnp.int32, (128, 1), 0) + i * 128)
        selt[pl.ds(i * 128, 128), :] = jnp.where(rows == lanes, 1.0, 0.0).astype(BF)
        return 0
    lax.fori_loop(0, 8, body, 0)
    acc[...] = jnp.zeros_like(acc)
    loss_acc[...] = jnp.zeros_like(loss_acc)
    tot_acc[...] = jnp.zeros_like(tot_acc)
    @pl.when(x < 3)
    def _():
        for k in (1, 7, 2, 6, 3, 5, 4):
            wz(rem(zl + k, 8), rem(zl + k, 8)).wait_recv()
        for k in (1, 3, 2):
            wx(rem(x + k, 4), x).start()

    def wy(yt, slot):
        return rc(wgat.at[slot, c], wgat.at[slot, c], wy_s.at[yt], wy_rs.at[slot], dev(x, zh, zl, yt, c))

    def wcc(slot, cc):
        return rc(wgat.at[slot, cc], wgat.at[slot, cc], wc_s.at[slot], wc_rs.at[slot], dev(x, zh, zl, y, oc))

    forward(1)
    for k in range(3):
        @pl.when(x != k)
        def _():
            wx(0, k).wait_recv()
    for k in (1, 3, 2):
        wy(rem(y + k, 4), y).start()
    wcc(y, c).start()
    forward(2)
    for k in (1, 3, 2):
        pcopy(rem(y + k, 4), rem(y + k, 4)).wait_recv()

    def body(i, _):
        pt[pl.ds(i * 256, 256), :] = nt(selt[pl.ds(i * 256, 256), :], pool[...].reshape(512, 768)).astype(BF)
        return 0
    lax.fori_loop(0, 4, body, 0)
    forward(3)
    for k in (1, 3, 2):
        wy(rem(y + k, 4), rem(y + k, 4)).wait_recv()
        wcc(rem(y + k, 4), c).start()
    forward(4)
    for k in (0, 1, 3, 2):
        wcc(rem(y + k, 4), oc).wait_recv()

    def body(i, _):
        wc[pl.ds(i * 256, 256), :] = nn(sel[pl.ds(i * 256, 256), :], wgat[...].reshape(1024, 768)).astype(BF)
        return 0
    lax.fori_loop(0, 3, body, 0)
    for n in range(3):
        iu[:, n * 256:(n + 1) * 256] = nn(pool[...].reshape(512, 768), wc[:, n * 256:(n + 1) * 256])

    def body(i, _):
        rows = pl.ds(i * 64, 64)
        pr = iu[rows, :]
        iv = lax.rsqrt(jnp.sum(pr * pr, axis=1, keepdims=True) + 1e-06)
        un = pr * iv
        iu[rows, :] = un
        inv[rows, :] = iv
        img[rows, :] = un.astype(BF)
        return 0
    lax.fori_loop(0, 8, body, 0)

    def compute(slot, own):
        pass
        for h in (0, 1):
            t_wait(slot, oc, h)
        tt = txt[slot].reshape(256, 768)
        s_scr[...] = nt(img[...], tt)

        def body(i, _):
            rows = pl.ds(i * 64, 64)
            scaled = s_scr[rows, :] * temp
            logit = scaled + bias
            if own:
                diag = (
                    lax.broadcasted_iota(jnp.int32, (64, 256), 0) + (i * 64 - y * 128)
                    == lax.broadcasted_iota(jnp.int32, (64, 256), 1) - c * 128
                ) & (lax.broadcasted_iota(jnp.int32, (64, 256), 1) // 128 == c)
                m = jnp.where(diag, -logit, logit)
            else:
                m = logit
            e = jnp.exp(-jnp.abs(m))
            u = 1.0 + e
            rcp = 1.0 / u
            lg = jnp.log(u) + (e - (u - 1.0)) * rcp
            soft = jnp.maximum(m, 0.0) + lg
            slope = jnp.where(m >= 0.0, 1.0, e) * rcp
            if own:
                slope = jnp.where(diag, -slope, slope)
            loss_acc[rows, :] += soft[:, 0:128] + soft[:, 128:256]
            sl = slope[:, 0:128] + slope[:, 128:256]
            st = slope * scaled
            st = st[:, 0:128] + st[:, 128:256]
            tot_acc[0] += jnp.sum(st.reshape(8, 8, 128), axis=0)
            tot_acc[1] += jnp.sum(sl.reshape(8, 8, 128), axis=0)
            slope_scr[rows, :] = slope.astype(BF)
            return 0
        lax.fori_loop(0, 8, body, 0)
        for n in range(3):
            acc[:, n * 256:(n + 1) * 256] += nn(slope_scr[...], tt[:, n * 256:(n + 1) * 256])

    forward(5)
    compute(zl, True)

    def both(d):
        def body(side, _):
            slot = zl + d * (2 * side - 1)

            @pl.when((slot >= 0) & (slot <= 7))
            def _():
                compute(slot, False)
            return 0
        lax.fori_loop(0, 2, body, 0)

    def body(d, _):
        @pl.when(d == 3)
        def _():
            forward(6)

        @pl.when(d == 6)
        def _():
            forward(7)
        both(d)
        return 0
    lax.fori_loop(1, 8, body, 0)

    def body(i, _):
        rows = pl.ds(i * 64, 64)
        gu = acc[rows, :] * temp
        un = iu[rows, :]
        g = ((gu - un * jnp.sum(un * gu, axis=1, keepdims=True)) * inv[rows, :]).astype(BF)
        gp[0, rows, :] = g[:, 0:384]
        gp[1, rows, :] = g[:, 384:768]
        return 0
    lax.fori_loop(0, 8, body, 0)
    def cchunk(j):
        return rc(cs.at[j], cbuf.at[j], c_s.at[j], c_rs.at[j], dev(x, zh, zl, y, oc))

    def body(k, _):
        j = rem(x + k, 4)
        cs[j] = nn(pt[pl.ds(j * 256, 256), :], gp[oc]).astype(BF)
        cchunk(j).start()
        return 0
    lax.fori_loop(1, 5, body, 0)

    def zcopy(to, slot):
        return rc(zs.at[:, to], zbuf.at[slot], z_s.at[to], z_rs.at[slot], dev(x, zh, to, y, c))

    me_xy = x * 4 + y

    def xycopy(xt, n, slot):
        return rc(xs.at[xt, n], xbuf.at[slot], x_s.at[xt, n], x_rs.at[slot], dev(xt, zh, zl, n, c))

    def body(k, _):
        j = rem(x + k, 4)
        mine = nn(pt[pl.ds(j * 256, 256), :], gp[c])
        cchunk(j).wait_recv()
        both_ = mine + cbuf[j].astype(F32)
        for n in range(3):
            xs[j, n] = both_[:, n * 128:(n + 1) * 128].astype(BF)

            @pl.when((k < 4) | (y != n))
            def _():
                xycopy(j, n, me_xy).start()
        return 0
    lax.fori_loop(1, 5, body, 0)

    @pl.when(y < 3)
    def _():
        xbuf[me_xy] = xs[x, y]

    for n in range(3):
        blk = wc[n * 256:(n + 1) * 256, :]
        fsend[:, :, n * 256:(n + 1) * 256] = (
            (nt(gp[0], blk[:, 0:384]) + nt(gp[1], blk[:, 384:768])).astype(BF).reshape(4, 128, 256)
        )

    def fcopy(yt, slot):
        return rc(fsend.at[yt], frecv.at[slot], f_s.at[yt], f_rs.at[slot], dev(x, zh, zl, yt, c))

    row = lax.broadcasted_iota(jnp.int32, (8, 128), 0)
    tl = jnp.sum(tot_acc[0], axis=0, keepdims=True)
    bl = jnp.sum(tot_acc[1], axis=0, keepdims=True)
    for j in range(4):
        part = jnp.sum(loss_acc[j * 128:(j + 1) * 128, :].T, axis=0, keepdims=True)
        lbuf[0, j] = jnp.where(row == 0, part, jnp.where(row == 1, tl, jnp.where(row == 2, bl, 0.0)))

    def lcopy(yt, slot):
        return rc(lbuf.at[0, yt], lbuf.at[1, slot], l_s.at[yt], l_rs.at[slot], dev(x, zh, zl, yt, c))

    for k in (1, 2, 3):
        lcopy(rem(y + k, 4), y).start()
    lbuf[1, y] = lbuf[0, y]
    for k in (1, 2, 3):
        lcopy(rem(y + k, 4), rem(y + k, 4)).wait_recv()
    ltot = lbuf[1, 0] + lbuf[1, 1] + lbuf[1, 2] + lbuf[1, 3]
    loss_ref[...] = ltot[0]
    me2 = zl * 2 + c
    s2buf[me2] = ltot

    def s2(to, slot):
        return rc(s2buf.at[me2], s2buf.at[slot], s2_s.at[to], s2_rs.at[slot], dev(x, zh, div(to, 2), y, rem(to, 2)))

    for k in range(1, 16):
        s2(rem(me2 + k, 16), me2).start()

    @pl.when(y < 3)
    def _():
        for k in range(1, 16):
            xycopy(0, 0, rem(me_xy + k, 16)).wait_recv()

        def body(i, _):
            rows = pl.ds(i * 64, 64)
            part = xbuf[0, rows, :].astype(F32)
            for k in range(1, 16):
                part = part + xbuf[k, rows, :].astype(F32)
            ysum[rows, :] = part.astype(BF)
            return 0
        lax.fori_loop(0, 4, body, 0)
        zs[...] = ysum[...].reshape(2, 8, 16, 128)
        for k in (4, 3, 5, 2, 6, 1, 7):
            zcopy(rem(zl + k, 8), zl).start()

    for k in (2, 1, 3):
        fcopy(rem(y + k, 4), y).start()

    for k in range(1, 16):
        s2(rem(me2 + k, 16), rem(me2 + k, 16)).wait_recv()
    s3buf[rep] = jnp.sum(s2buf[...], axis=0)

    def s3(to, slot):
        return rc(s3buf.at[rep], s3buf.at[slot], s3_s.at[to], s3_rs.at[slot], (to, zero))

    for k in range(1, 8):
        s3(rem(rep + k, 8), rep).start()

    def acopy(k, j, h):
        return rc(
            agb.at[rem(k, 2)], abuf.at[h, j], a_s.at[k], a_rs.at[h, j],
            dev(div(k, 4), rem(div(k, 2), 2), zl, x, rem(k, 2)),
        )

    me_a = c * 3 + y

    @pl.when(y < 3)
    def _():
        zbuf[zl] = zs[:, zl]
        for k in (1, 7, 2, 6, 3, 5, 4):
            zcopy(rem(zl + k, 8), rem(zl + k, 8)).wait_recv()
        agb[...] = jnp.sum(zbuf[...].astype(F32), axis=0).astype(BF)

        def body(k, _):
            @pl.when(jnp.logical_not(ag_self(k)))
            def _():
                acopy(k, me_a, zh).start()
            return 0
        lax.fori_loop(0, 16, body, 0)

        @pl.when(x == y)
        def _():
            abuf[zh, me_a] = agb[c]

    for k in (1, 3, 2):
        fcopy(rem(y + k, 4), rem(y + k, 4)).wait_recv()
    frecv[y] = fsend[y]
    feat_ref[...] = (
        frecv[0].astype(F32) + frecv[1].astype(F32) + frecv[2].astype(F32) + frecv[3].astype(F32)
    ).astype(BF)

    for k in range(1, 8):
        s3(rem(rep + k, 8), rem(rep + k, 8)).wait_recv()
    fin = jnp.sum(s3buf[...], axis=0)
    sc_ref[0] = jnp.sum(fin[1:2, :])
    sc_ref[1] = jnp.sum(fin[2:3, :])

    @pl.when(x < 3)
    def _():
        for k in range(1, 8):
            wz(rem(zl + k, 8), zl).wait_send()
        for k in (1, 2, 3):
            wx(rem(x + k, 4), x).wait_send()
    for k in (1, 2, 3):
        pass
        pcopy(rem(y + k, 4), y).wait_send()
        wy(rem(y + k, 4), y).wait_send()
        fcopy(rem(y + k, 4), y).wait_send()
        lcopy(rem(y + k, 4), y).wait_send()
    for n in range(3):
        for k in (1, 2, 3):
            xycopy(rem(x + k, 4), n, me_xy).wait_send()

        @pl.when(y != n)
        def _():
            xycopy(x, n, me_xy).wait_send()
    for k in range(4):
        pass
        wcc(k, c).wait_send()
        cchunk(k).wait_send()

    def body(slot, _):
        for h in (0, 1):
            t_sib(slot, h).wait_send()

            @pl.when((slot <= zl) & (zl < 7))
            def _():
                t_right(slot, h).wait_send()

            @pl.when((slot >= zl) & (zl > 0))
            def _():
                t_left(slot, h).wait_send()
        return 0
    lax.fori_loop(0, 8, body, 0)
    for k in range(1, 16):
        s2(rem(me2 + k, 16), me2).wait_send()
    for k in range(1, 8):
        s3(rem(rep + k, 8), rep).wait_send()

    @pl.when(y < 3)
    def _():
        for k in range(1, 8):
            zcopy(rem(zl + k, 8), zl).wait_send()

    def body(k, _):
        @pl.when(jnp.logical_not(ag_from_self(k)))
        def _():
            acopy(0, rem(k, 2) * 3 + div(k, 4), rem(div(k, 2), 2)).wait_recv()
        return 0
    lax.fori_loop(0, 12, body, 0)
    for j in range(6):
        wg_ref[:, j * 128:(j + 1) * 128] = (abuf[0, j].astype(F32) + abuf[1, j].astype(F32))[0:12, :]

    @pl.when(y < 3)
    def _():
        def body(k, _):
            @pl.when(jnp.logical_not(ag_self(k)))
            def _():
                acopy(k, me_a, zh).wait_send()
            return 0
        lax.fori_loop(0, 16, body, 0)


def hand_out(loss_in, feat_in, wg_in, sc_in, loss_out, feat_out, wg_out, sc_out):
    loss_out[...] = loss_in[...]
    feat_out[...] = feat_in[...]
    wg_out[...] = wg_in[...]
    sc_out[0] = sc_in[0]
    sc_out[1] = sc_in[1]


def per_device(pooled, text_embed, head_weight, natural_exponent_factor, logit_bias):
    vm = pl.BlockSpec(memory_space=pltpu.VMEM)
    sm = pl.BlockSpec(memory_space=pltpu.SMEM)
    V = pltpu.VMEM
    D = pltpu.SemaphoreType.DMA
    loss, feat, wgrad, sc = pl.pallas_call(
        kernel,
        out_shape=(
            jax.ShapeDtypeStruct((128,), F32),
            jax.ShapeDtypeStruct((128, 768), BF),
            jax.ShapeDtypeStruct((12, 768), F32),
            jax.ShapeDtypeStruct((2,), F32),
        ),
        in_specs=[vm, vm, vm, sm, sm],
        out_specs=(vm, vm, vm, sm),
        scratch_shapes=[
            V((8, 2, 128, 768), BF), V((4, 128, 768), BF), V((4, 2, 8, 16, 768), BF),
            V((768, 1024), BF), V((1024, 768), BF), V((768, 768), BF), V((1024, 512), BF),
            V((512, 768), F32), V((512, 1), F32), V((512, 768), BF), V((512, 256), F32), V((512, 256), BF),
            V((512, 768), F32), V((512, 128), F32), V((2, 8, 128), F32),
            V((2, 512, 384), BF), V((4, 128, 768), BF), V((4, 128, 768), BF), V((2, 4, 8, 128), F32),
            V((4, 256, 384), BF), V((4, 256, 384), BF), V((4, 3, 256, 128), BF), V((16, 256, 128), BF), V((256, 128), BF),
            V((2, 8, 16, 128), BF), V((8, 2, 16, 128), BF), V((2, 16, 128), BF), V((2, 6, 16, 128), BF),
            V((16, 8, 128), F32), V((8, 8, 128), F32),
            D((8, 2, 2)), D((8, 2)), D((8, 2)), D((8, 2)), D((4,)), D((4,)),
            D((8,)), D((8,)), D((4,)), D((4,)), D((4,)), D((4,)), D((4,)), D((4,)),
            D((4,)), D((4,)), D((4,)), D((4,)), D((4,)), D((4,)), D((16,)), D((4, 3)),
            D((8,)), D((8,)), D((2, 6)), D((16,)), D((16,)), D((16,)), D((8,)), D((8,)),
        ],
        compiler_params=pltpu.CompilerParams(
            collective_id=0, has_side_effects=True, vmem_limit_bytes=56 << 20
        ),
    )(pooled, text_embed, head_weight, natural_exponent_factor, logit_bias)
    return pl.pallas_call(
        hand_out,
        out_shape=(
            jax.ShapeDtypeStruct((128,), F32),
            jax.ShapeDtypeStruct((128, 768), BF),
            jax.ShapeDtypeStruct((12, 768), F32),
            jax.ShapeDtypeStruct((2,), F32),
        ),
        in_specs=[vm, vm, vm, sm],
        out_specs=(vm, vm, vm, sm),
    )(loss, feat, wgrad, sc)


def solution(mesh):
    return jax.shard_map(
        per_device,
        mesh=mesh,
        in_specs=(P(("rep", "zero"), None), P(("rep", "zero"), None), P("zero", None), P(), P()),
        out_specs=(P(("rep", "zero")), P(("rep", "zero"), None), P("zero", None), P()),
        check_vma=False,
    )
```

time: 918 us -> 100 us (0.11)
  blocking collectives: 622 us -> 0 us
  waiting for transfers between devices: 253 us -> 0 us
  Pallas kernels: 0 us -> 98.1 us
  matrix products: 18.2 us -> 0 us
  between operations: 16.1 us -> 1.93 us
    unnamed x1 -> x0, blocking collectives: 439 us -> none
    all_gather x2 -> x0, waiting for transfers between devices: 252 us -> none  [the longest x1 130 us: per_device(): portion_ratio = lax.all_gather(txt_bf, 'zero', axis=0, tiled=True)]
    psum x2 -> x0, blocking collectives: 182 us -> none  [the longest x1 112 us: per_device(): scale_grads = lax.psum(jnp.stack([temp_part, bias_part]), ('rep', 'zero'))]
    pallas_call x0 -> x2, Pallas kernels: none -> 98.1 us  [the longest x1 96.4 us: per_device(): pl.pallas_call(kernel, out_shape=(jax.ShapeDtypeStruct((128,), F32), jax....]
    dot_general x5 -> x0, matrix products: 18.2 us -> none  [the longest x1 11.6 us: patch_penalty_entries(): lax.dot_general(picture_sample_slab, caption_sample_slab, (((1,), (1,)),...]
  transfers between devices with their start and end apart: 2 -> 0, of which waited for: 2 -> 0; matrix products, arithmetic and copies ran while one was open for 1% -> 0% of each run, Pallas kernels for 0% -> 0%
where the time goes in v1:
time: 100 us
  Pallas kernels  98.1 us (98%)
  between operations  1.93 us (2%)
    pallas_call x1, Pallas kernels, per_device(): pl.pallas_call(kernel, out_shape=(jax.ShapeDtypeStruct((128,), F32), jax....  96.4 us

profile of v1, /device:TPU:1, one launch (start us, length us, event | category | flops | bytes accessed | tf_op | source)
XLA Modules:
  0.0 100.0 jit_solution(15434127460403888865)
XLA Ops:
  1.9 96.4 %shard_map.84 = (f32[128]{0:T(128)}, bf16[128,768]{1,0:T(8,128)(2,1)}, f32[12,768]{1,0:T(8,128)}, f32[2]{0:T(128)}) custom-call(bf16[128,768]{1,0:T(8,128)(2,1)} %p_ref.1, bf16[128,768]{1,0:T(8,128)(2,1)} %t_ref.1, bf16[12,768]{1,0:T(8,128)(2,1)} %w_ref.1, f32[1]{0:T(128)S(6)} %copy.9.nat_ref, f32[1]{0:T(128)S(6)} %copy.10.bias_ref), custom_call_target="tpu_custom_call" | custom-call | tf_op jit(solution)/shard_map/pallas_call | solution.py:513
  98.4 1.7 %shard_map.85 = (f32[128]{0:T(128)}, bf16[128,768]{1,0:T(8,128)(2,1)}, f32[12,768]{1,0:T(8,128)}, f32[2]{0:T(128)}) custom-call(f32[128]{0:T(128)} %get-tuple-element.8.loss_in, bf16[128,768]{1,0:T(8,128)(2,1)} %get-tuple-element.9.feat_in, f32[12,768]{1,0:T(8,128)} %get-tuple-element.10.wg_in, f32[2]{0:T(128)} %get-tuple-element.11.sc_in), custom_call_target="tpu_custom_call" | custom-call | tf_op jit(solution)/shard_map/pallas_call | solution.py:541

commit v2 on v1

--- a/solution.py
+++ b/solution.py
@@ -33,10 +33,10 @@
 def kernel(
     p_ref, t_ref, w_ref, nat_ref, bias_ref,
     loss_ref, feat_ref, wg_ref, sc_ref,
-    txt, pool, wgat, sel, selt, wc, pt, iu, inv, img, s_scr, slope_scr, acc, loss_acc, tot_acc,
-    gp, fsend, frecv, lbuf, cs, cbuf, xs, xbuf, ysum, zs, zbuf, agb, abuf, s2buf, s3buf,
+    txt, pool, wgat, w2, sel, selt, wc, pt, iu, inv, img, s_scr, slope_scr, acc, loss_acc, tot_acc,
+    gp, fsend, frecv, lbuf, cs, cbuf, xs, xbuf, ys, ybuf, ysum, zs, zbuf, agb, abuf, s2buf, s3buf,
     t_rs, t_sr, t_sl, t_ss, p_rs, p_s, wz_rs, wz_s, wx_rs, wx_s, wy_rs, wy_s, wc_rs, wc_s,
-    f_rs, f_s, l_rs, l_s, c_rs, c_s, x_rs, x_s, z_rs, z_s, a_rs, a_s, s2_rs, s2_s, s3_rs, s3_s,
+    f_rs, f_s, l_rs, l_s, c_rs, c_s, x_rs, x_s, y_rs, y_s, z_rs, z_s, a_rs, a_s, s2_rs, s2_s, s3_rs, s3_s,
 ):
     rep = lax.axis_index("rep")
     zero = lax.axis_index("zero")
@@ -65,12 +65,6 @@
         sig(dev(x, zh, rem(zl + k, 8), y, c))
     sig(dev(x, 1 - zh, zl, y, c))
 
-    def ag_self(k):
-        return (div(k, 4) == x) & (rem(div(k, 2), 2) == zh) & (x == y) & (rem(k, 2) == c)
-
-    def ag_from_self(k):
-        return (x == y) & (div(k, 4) == y) & (rem(div(k, 2), 2) == zh) & (rem(k, 2) == c)
-
     tf = t_ref[...].astype(F32)
     txt[zl, c] = (tf * lax.rsqrt(jnp.sum(tf * tf, axis=1, keepdims=True) + 1e-06)).astype(BF)
     pl.semaphore_wait(bar, 18)
@@ -146,7 +140,11 @@
         r = k % 16
         return jnp.where(r < 12, 96 * ((k // 16) % 8) + 12 * (k // 128) + r, -1)
 
-    cols = where_row(lax.broadcasted_iota(jnp.int32, (1, 1024), 1))
+    slots = lax.broadcasted_iota(jnp.int32, (1, 128), 1)
+    slots = jnp.where(slots % 16 < 12, 12 * (slots // 16) + slots % 16, -1)
+    csel = jnp.where(lax.broadcasted_iota(jnp.int32, (96, 1), 0) == slots, 1.0, 0.0).astype(BF)
+    cols = lax.broadcasted_iota(jnp.int32, (1, 768), 1)
+    cols = 96 * ((cols % 96) // 12) + 12 * (cols // 96) + cols % 12
 
     def body(i, _):
         rows = lax.broadcasted_iota(jnp.int32, (128, 1), 0) + i * 128
@@ -171,16 +169,17 @@
             wx(rem(x + k, 4), x).start()
 
     def wy(yt, slot):
-        return rc(wgat.at[slot, c], wgat.at[slot, c], wy_s.at[yt], wy_rs.at[slot], dev(x, zh, zl, yt, c))
+        return rc(w2.at[slot, c], w2.at[slot, c], wy_s.at[yt], wy_rs.at[slot], dev(x, zh, zl, yt, c))
 
     def wcc(slot, cc):
-        return rc(wgat.at[slot, cc], wgat.at[slot, cc], wc_s.at[slot], wc_rs.at[slot], dev(x, zh, zl, y, oc))
+        return rc(w2.at[slot, cc], w2.at[slot, cc], wc_s.at[slot], wc_rs.at[slot], dev(x, zh, zl, y, oc))
 
     forward(1)
     for k in range(3):
         @pl.when(x != k)
         def _():
             wx(0, k).wait_recv()
+    w2[y, c] = nn(csel, wgat[y, c].reshape(128, 768)).astype(BF)
     for k in (1, 3, 2):
         wy(rem(y + k, 4), y).start()
     wcc(y, c).start()
@@ -196,12 +195,11 @@
     for k in (1, 3, 2):
         wy(rem(y + k, 4), rem(y + k, 4)).wait_recv()
         wcc(rem(y + k, 4), c).start()
-    forward(4)
     for k in (0, 1, 3, 2):
         wcc(rem(y + k, 4), oc).wait_recv()
 
     def body(i, _):
-        wc[pl.ds(i * 256, 256), :] = nn(sel[pl.ds(i * 256, 256), :], wgat[...].reshape(1024, 768)).astype(BF)
+        wc[pl.ds(i * 256, 256), :] = nn(sel[pl.ds(i * 256, 256), :], w2[...].reshape(768, 768)).astype(BF)
         return 0
     lax.fori_loop(0, 3, body, 0)
     for n in range(3):
@@ -257,7 +255,7 @@
         for n in range(3):
             acc[:, n * 256:(n + 1) * 256] += nn(slope_scr[...], tt[:, n * 256:(n + 1) * 256])
 
-    forward(5)
+    forward(4)
     compute(zl, True)
 
     def both(d):
@@ -271,13 +269,9 @@
         lax.fori_loop(0, 2, body, 0)
 
     def body(d, _):
-        @pl.when(d == 3)
-        def _():
-            forward(6)
-
-        @pl.when(d == 6)
-        def _():
-            forward(7)
+        @pl.when((d == 2) | (d == 4) | (d == 7))
+        def _():
+            forward(jnp.where(d == 2, 5, jnp.where(d == 4, 6, 7)))
         both(d)
         return 0
     lax.fori_loop(1, 8, body, 0)
@@ -295,7 +289,7 @@
         return rc(cs.at[j], cbuf.at[j], c_s.at[j], c_rs.at[j], dev(x, zh, zl, y, oc))
 
     def body(k, _):
-        j = rem(x + k, 4)
+        j = rem(jnp.where(c == 0, y, x) + k, 4)
         cs[j] = nn(pt[pl.ds(j * 256, 256), :], gp[oc]).astype(BF)
         cchunk(j).start()
         return 0
@@ -304,28 +298,29 @@
     def zcopy(to, slot):
         return rc(zs.at[:, to], zbuf.at[slot], z_s.at[to], z_rs.at[slot], dev(x, zh, to, y, c))
 
-    me_xy = x * 4 + y
-
-    def xycopy(xt, n, slot):
-        return rc(xs.at[xt, n], xbuf.at[slot], x_s.at[xt, n], x_rs.at[slot], dev(xt, zh, zl, n, c))
+    fst, snd = jnp.where(c == 0, x, y), jnp.where(c == 0, y, x)
+
+    def place(f, g):
+        return dev(jnp.where(c == 0, f, g), zh, zl, jnp.where(c == 0, g, f), c)
+
+    def xcopy(to, slot):
+        return rc(xs.at[to], xbuf.at[slot], x_s.at[to], x_rs.at[slot], place(to, snd))
+
+    def ycopy(to, slot):
+        return rc(ys.at[to], ybuf.at[slot], y_s.at[to], y_rs.at[slot], place(fst, to))
 
     def body(k, _):
-        j = rem(x + k, 4)
+        j = rem(fst + k, 4)
         mine = nn(pt[pl.ds(j * 256, 256), :], gp[c])
         cchunk(j).wait_recv()
-        both_ = mine + cbuf[j].astype(F32)
-        for n in range(3):
-            xs[j, n] = both_[:, n * 128:(n + 1) * 128].astype(BF)
-
-            @pl.when((k < 4) | (y != n))
-            def _():
-                xycopy(j, n, me_xy).start()
+        xs[j] = (mine + cbuf[j].astype(F32)).astype(BF)
+
+        @pl.when(k < 4)
+        def _():
+            xcopy(j, fst).start()
         return 0
     lax.fori_loop(1, 5, body, 0)
-
-    @pl.when(y < 3)
-    def _():
-        xbuf[me_xy] = xs[x, y]
+    xbuf[fst] = xs[fst]
 
     for n in range(3):
         blk = wc[n * 256:(n + 1) * 256, :]
@@ -362,25 +357,37 @@
     for k in range(1, 16):
         s2(rem(me2 + k, 16), me2).start()
 
-    @pl.when(y < 3)
-    def _():
-        for k in range(1, 16):
-            xycopy(0, 0, rem(me_xy + k, 16)).wait_recv()
-
-        def body(i, _):
-            rows = pl.ds(i * 64, 64)
-            part = xbuf[0, rows, :].astype(F32)
-            for k in range(1, 16):
-                part = part + xbuf[k, rows, :].astype(F32)
-            ysum[rows, :] = part.astype(BF)
-            return 0
-        lax.fori_loop(0, 4, body, 0)
+    for k in (1, 3, 2):
+        xcopy(0, rem(fst + k, 4)).wait_recv()
+
+    def body(i, _):
+        rows = pl.ds(i * 64, 64)
+        part = xbuf[0, rows, :].astype(F32)
+        for k in range(1, 4):
+            part = part + xbuf[k, rows, :].astype(F32)
+        for n in range(3):
+            ys[n, rows, :] = part[:, n * 128:(n + 1) * 128].astype(BF)
+        return 0
+    lax.fori_loop(0, 4, body, 0)
+    for n in range(3):
+        @pl.when(snd != n)
+        def _():
+            ycopy(n, snd).start()
+    for k in (2, 1, 3):
+        fcopy(rem(y + k, 4), y).start()
+
+    @pl.when(snd < 3)
+    def _():
+        ybuf[snd] = ys[snd]
+        for k in (1, 3, 2):
+            ycopy(0, rem(snd + k, 4)).wait_recv()
+        ysum[...] = (
+            ybuf[0].astype(F32) + ybuf[1].astype(F32) + ybuf[2].astype(F32) + ybuf[3].astype(F32)
+        ).astype(BF)
         zs[...] = ysum[...].reshape(2, 8, 16, 128)
         for k in (4, 3, 5, 2, 6, 1, 7):
             zcopy(rem(zl + k, 8), zl).start()
 
-    for k in (2, 1, 3):
-        fcopy(rem(y + k, 4), y).start()
 
     for k in range(1, 16):
         s2(rem(me2 + k, 16), rem(me2 + k, 16)).wait_recv()
@@ -392,15 +399,21 @@
     for k in range(1, 8):
         s3(rem(rep + k, 8), rep).start()
 
+    def ag_self(k):
+        return (div(k, 4) == x) & (rem(div(k, 2), 2) == zh) & (fst == y) & (rem(k, 2) == c)
+
+    def ag_from_self(k):
+        return (fst == y) & (div(k, 4) == snd) & (rem(div(k, 2), 2) == zh) & (rem(k, 2) == c)
+
     def acopy(k, j, h):
         return rc(
             agb.at[rem(k, 2)], abuf.at[h, j], a_s.at[k], a_rs.at[h, j],
-            dev(div(k, 4), rem(div(k, 2), 2), zl, x, rem(k, 2)),
+            dev(div(k, 4), rem(div(k, 2), 2), zl, fst, rem(k, 2)),
         )
 
-    me_a = c * 3 + y
-
-    @pl.when(y < 3)
+    me_a = c * 3 + snd
+
+    @pl.when(snd < 3)
     def _():
         zbuf[zl] = zs[:, zl]
         for k in (1, 7, 2, 6, 3, 5, 4):
@@ -414,7 +427,7 @@
             return 0
         lax.fori_loop(0, 16, body, 0)
 
-        @pl.when(x == y)
+        @pl.when(fst == y)
         def _():
             abuf[zh, me_a] = agb[c]
 
@@ -443,13 +456,12 @@
         wy(rem(y + k, 4), y).wait_send()
         fcopy(rem(y + k, 4), y).wait_send()
         lcopy(rem(y + k, 4), y).wait_send()
+    for k in (1, 2, 3):
+        xcopy(rem(fst + k, 4), fst).wait_send()
     for n in range(3):
-        for k in (1, 2, 3):
-            xycopy(rem(x + k, 4), n, me_xy).wait_send()
-
-        @pl.when(y != n)
-        def _():
-            xycopy(x, n, me_xy).wait_send()
+        @pl.when(snd != n)
+        def _():
+            ycopy(n, snd).wait_send()
     for k in range(4):
         pass
         wcc(k, c).wait_send()
@@ -473,7 +485,7 @@
     for k in range(1, 8):
         s3(rem(rep + k, 8), rep).wait_send()
 
-    @pl.when(y < 3)
+    @pl.when(snd < 3)
     def _():
         for k in range(1, 8):
             zcopy(rem(zl + k, 8), zl).wait_send()
@@ -487,7 +499,7 @@
     for j in range(6):
         wg_ref[:, j * 128:(j + 1) * 128] = (abuf[0, j].astype(F32) + abuf[1, j].astype(F32))[0:12, :]
 
-    @pl.when(y < 3)
+    @pl.when(snd < 3)
     def _():
         def body(k, _):
             @pl.when(jnp.logical_not(ag_self(k)))
@@ -521,17 +533,17 @@
         in_specs=[vm, vm, vm, sm, sm],
         out_specs=(vm, vm, vm, sm),
         scratch_shapes=[
-            V((8, 2, 128, 768), BF), V((4, 128, 768), BF), V((4, 2, 8, 16, 768), BF),
-            V((768, 1024), BF), V((1024, 768), BF), V((768, 768), BF), V((1024, 512), BF),
+            V((8, 2, 128, 768), BF), V((4, 128, 768), BF), V((4, 2, 8, 16, 768), BF), V((4, 2, 96, 768), BF),
+            V((768, 768), BF), V((1024, 768), BF), V((768, 768), BF), V((1024, 512), BF),
             V((512, 768), F32), V((512, 1), F32), V((512, 768), BF), V((512, 256), F32), V((512, 256), BF),
             V((512, 768), F32), V((512, 128), F32), V((2, 8, 128), F32),
             V((2, 512, 384), BF), V((4, 128, 768), BF), V((4, 128, 768), BF), V((2, 4, 8, 128), F32),
-            V((4, 256, 384), BF), V((4, 256, 384), BF), V((4, 3, 256, 128), BF), V((16, 256, 128), BF), V((256, 128), BF),
+            V((4, 256, 384), BF), V((4, 256, 384), BF), V((4, 256, 384), BF), V((4, 256, 384), BF), V((3, 256, 128), BF), V((4, 256, 128), BF), V((256, 128), BF),
             V((2, 8, 16, 128), BF), V((8, 2, 16, 128), BF), V((2, 16, 128), BF), V((2, 6, 16, 128), BF),
             V((16, 8, 128), F32), V((8, 8, 128), F32),
             D((8, 2, 2)), D((8, 2)), D((8, 2)), D((8, 2)), D((4,)), D((4,)),
             D((8,)), D((8,)), D((4,)), D((4,)), D((4,)), D((4,)), D((4,)), D((4,)),
-            D((4,)), D((4,)), D((4,)), D((4,)), D((4,)), D((4,)), D((16,)), D((4, 3)),
+            D((4,)), D((4,)), D((4,)), D((4,)), D((4,)), D((4,)), D((4,)), D((4,)), D((4,)), D((4,)),
             D((8,)), D((8,)), D((2, 6)), D((16,)), D((16,)), D((16,)), D((8,)), D((8,)),
         ],
         compiler_params=pltpu.CompilerParams(

time: 100 us -> 98 us (0.980)
  Pallas kernels: 98.1 us -> 95.9 us
    pallas_call x1, Pallas kernels: 96.4 us -> 94.3 us  [per_device(): pl.pallas_call(kernel, out_shape=(jax.ShapeDtypeStruct((128,), F32), jax....]
where the time goes in v2:
time: 98 us; the launch traced here: 97.9 us
  Pallas kernels  95.9 us (98%)
  between operations  1.93 us (2%)
    pallas_call x1, Pallas kernels, per_device(): pl.pallas_call(kernel, out_shape=(jax.ShapeDtypeStruct((128,), F32), jax....  94.3 us

profile of v2, /device:TPU:1, one launch (start us, length us, event | category | flops | bytes accessed | tf_op | source)
XLA Modules:
  0.0 97.9 jit_solution(7996293590433039087)
XLA Ops:
  1.9 94.3 %shard_map.84 = (f32[128]{0:T(128)}, bf16[128,768]{1,0:T(8,128)(2,1)}, f32[12,768]{1,0:T(8,128)}, f32[2]{0:T(128)}) custom-call(bf16[128,768]{1,0:T(8,128)(2,1)} %p_ref.1, bf16[128,768]{1,0:T(8,128)(2,1)} %t_ref.1, bf16[12,768]{1,0:T(8,128)(2,1)} %w_ref.1, f32[1]{0:T(128)S(6)} %copy.9.nat_ref, f32[1]{0:T(128)S(6)} %copy.10.bias_ref), custom_call_target="tpu_custom_call" | custom-call | tf_op jit(solution)/shard_map/pallas_call | solution.py:525
  96.2 1.7 %shard_map.85 = (f32[128]{0:T(128)}, bf16[128,768]{1,0:T(8,128)(2,1)}, f32[12,768]{1,0:T(8,128)}, f32[2]{0:T(128)}) custom-call(f32[128]{0:T(128)} %get-tuple-element.8.loss_in, bf16[128,768]{1,0:T(8,128)(2,1)} %get-tuple-element.9.feat_in, f32[12,768]{1,0:T(8,128)} %get-tuple-element.10.wg_in, f32[2]{0:T(128)} %get-tuple-element.11.sc_in), custom_call_target="tpu_custom_call" | custom-call | tf_op jit(solution)/shard_map/pallas_call | solution.py:553

commit v3 on v2

--- a/solution.py
+++ b/solution.py
@@ -255,8 +255,8 @@
         for n in range(3):
             acc[:, n * 256:(n + 1) * 256] += nn(slope_scr[...], tt[:, n * 256:(n + 1) * 256])
 
+    compute(zl, True)
     forward(4)
-    compute(zl, True)
 
     def both(d):
         def body(side, _):

time: 98 us -> 99.5 us (1.015)
  Pallas kernels: 95.9 us -> 97.4 us
    pallas_call x1, Pallas kernels: 94.3 us -> 95.7 us  [per_device(): pl.pallas_call(kernel, out_shape=(jax.ShapeDtypeStruct((128,), F32), jax....]
where the time goes in v3:
time: 99.5 us; the launch traced here: 99.3 us
  Pallas kernels  97.4 us (98%)
  between operations  1.93 us (2%)
    pallas_call x1, Pallas kernels, per_device(): pl.pallas_call(kernel, out_shape=(jax.ShapeDtypeStruct((128,), F32), jax....  95.7 us

profile of v3, /device:TPU:1, one launch (start us, length us, event | category | flops | bytes accessed | tf_op | source)
XLA Modules:
  0.0 99.3 jit_solution(18440855319153089727)
XLA Ops:
  1.9 95.7 %shard_map.84 = (f32[128]{0:T(128)}, bf16[128,768]{1,0:T(8,128)(2,1)}, f32[12,768]{1,0:T(8,128)}, f32[2]{0:T(128)}) custom-call(bf16[128,768]{1,0:T(8,128)(2,1)} %p_ref.1, bf16[128,768]{1,0:T(8,128)(2,1)} %t_ref.1, bf16[12,768]{1,0:T(8,128)(2,1)} %w_ref.1, f32[1]{0:T(128)S(6)} %copy.9.nat_ref, f32[1]{0:T(128)S(6)} %copy.10.bias_ref), custom_call_target="tpu_custom_call" | custom-call | tf_op jit(solution)/shard_map/pallas_call | solution.py:525
  97.6 1.7 %shard_map.85 = (f32[128]{0:T(128)}, bf16[128,768]{1,0:T(8,128)(2,1)}, f32[12,768]{1,0:T(8,128)}, f32[2]{0:T(128)}) custom-call(f32[128]{0:T(128)} %get-tuple-element.8.loss_in, bf16[128,768]{1,0:T(8,128)(2,1)} %get-tuple-element.9.feat_in, f32[12,768]{1,0:T(8,128)} %get-tuple-element.10.wg_in, f32[2]{0:T(128)} %get-tuple-element.11.sc_in), custom_call_target="tpu_custom_call" | custom-call | tf_op jit(solution)/shard_map/pallas_call | solution.py:553
